TPU v7x, 32 devices: a whole 2x2x4 slice. The times are simulated.
32 devices in a mesh: replica: 2 (over y), head: 8 (over z, x), batch: 2 (over core).
Axes of the slice: x: 2, y: 2, z: 4, core: 2. Of those that a mesh axis runs over, the one named last changes fastest.
Arguments:
- residual: bfloat16 [2, 16, 8192], P(None, ('replica', 'batch'), 'head'), parts along dimension 1, may hold values from -4.5 to 4.5
- norm_gain: bfloat16 [8192], P('head'), may hold values from 0.099609375 to 1.8984375
- queries: bfloat16 [2, 32, 4, 8, 128], P(None, ('replica', 'batch', 'head')), parts along dimension 1, may hold values from -140 to 140
- cache_keys: bfloat16 [2, 32, 4, 256, 128], P(None, ('replica', 'batch', 'head')), parts along dimension 1, may hold values from -6 to 6
- cache_values: bfloat16 [2, 32, 4, 256, 128], P(None, ('replica', 'batch', 'head')), parts along dimension 1, may hold values from -6 to 6
- new_keys: bfloat16 [2, 32, 4, 128], P(None, ('replica', 'batch', 'head')), parts along dimension 1, may hold values from -6 to 6
- new_values: bfloat16 [2, 32, 4, 128], P(None, ('replica', 'batch', 'head')), parts along dimension 1, may hold values from -6 to 6
- lengths: int32 [2, 16], P(None, 'replica'), parts along dimension 1, may hold values from 64 to 256, as said below
- out_packed: int32 [4096, 8192], P(None, 'head'), may hold values from 0 to 255
- out_scales: bfloat16 [64, 8192], P(None, 'head'), may hold values from 0.0012130737 to 0.004852295
- ffn_packed: int32 [8192, 32768], P('batch', 'head'), may hold values from 0 to 4095
- gate_scales: bfloat16 [64, 32768], P('batch', 'head'), may hold values from 0.0012130737 to 0.004852295
- up_scales: bfloat16 [64, 32768], P('batch', 'head'), may hold values from 0.0012130737 to 0.004852295
- down_scales: bfloat16 [256, 8192], P('head', 'batch'), may hold values from 0.00060653687 to 0.0024261475
Outputs:
- attn_stream: bfloat16 [2, 16, 8192], P(None, ('replica', 'batch'), 'head'), parts along dimension 1
- ffn_out: bfloat16 [2, 16, 8192], P(None, 'replica', ('batch', 'head')), parts along dimension 1
There are 2 independent parts, one for each index of `replica`. A program takes and returns all parts, laid end to end along the dimension named above; an argument that names none is the same for every part. Nothing has to cross between parts.
Inputs may be any that keep to these rules, and one draw needn't show every extreme that they name: `lengths`: the first sequence of each micro-batch holds all 256 positions.
All inputs are finite; a program needn't handle non-finite values.
Results may differ from a plain program's by a relative error of at most 0.0065.
Values may be sent and summed in bfloat16 or wider, within the bound.
A program may use at most 384 MiB of HBM per device.

v0:
```python
import jax
import jax.numpy as jnp
from jax import lax
from jax.sharding import PartitionSpec as P

KV_HEADS = 8


epsilon = 1e-05


def unpack_pairs(packed, scales):
    shifts = 4 * jnp.arange(2, dtype=jnp.int32)
    nibbles = jnp.bitwise_and(jnp.right_shift(packed[:, None, :], shifts[None, :, None]), 15)
    nibbles = nibbles.reshape(packed.shape[0] * 2, packed.shape[1]).astype(jnp.float32) - 8.0
    spread = jnp.repeat(scales.astype(jnp.float32), nibbles.shape[0] // scales.shape[0], axis=0)
    return (nibbles * spread).astype(jnp.bfloat16)


def field_codes(words, shift, scales):
    nibbles = jnp.bitwise_and(jnp.right_shift(words, shift), 15).astype(jnp.float32) - 8.0
    spread = jnp.repeat(scales.astype(jnp.float32), words.shape[0] // scales.shape[0], axis=0)
    return (nibbles * spread).astype(jnp.bfloat16)


def attend(query, keys, values, key_new, value_new, seq_lens, scale):
    scores = jnp.einsum("ske,spe->skp", query, keys, preferred_element_type=jnp.float32) * scale
    score_new = jnp.einsum("ske,se->sk", query, key_new, preferred_element_type=jnp.float32) * scale
    position = jnp.arange(keys.shape[1], dtype=jnp.int32)
    live_mask = position[None, None, :] < seq_lens[:, None, None]
    row_max = jnp.maximum(jnp.max(jnp.where(live_mask, scores, -jnp.inf), axis=-1), score_new)
    weights = jnp.where(live_mask, jnp.exp(scores - row_max[..., None]), 0.0)
    weight_new = jnp.exp(score_new - row_max)
    denominator = jnp.sum(weights, axis=-1) + weight_new
    probs = (weights / denominator[..., None]).astype(jnp.bfloat16)
    prob_new = (weight_new / denominator).astype(jnp.bfloat16)
    mixed = jnp.einsum("skp,spe->ske", probs, values, preferred_element_type=jnp.float32)
    mixed = (
        mixed + prob_new.astype(jnp.float32)[..., None] * value_new.astype(jnp.float32)[:, None, :]
    )
    return mixed.astype(jnp.bfloat16).reshape(mixed.shape[0], -1)


def body(
    residual,
    norm_gain,
    queries,
    cache_keys,
    cache_values,
    new_keys,
    new_values,
    lengths,
    out_packed,
    out_scales,
    ffn_packed,
    gate_scales,
    up_scales,
    down_scales,
):
    micro_count = queries.shape[0]
    seq_dev = queries.shape[2]
    scale = queries.shape[4] ** (-0.5)
    unit = lax.axis_index("batch") * lax.axis_size("head") + lax.axis_index("head")
    first_row = unit // KV_HEADS * seq_dev
    out_weight = unpack_pairs(out_packed, out_scales)
    width_out = out_weight.shape[1]
    out_weight = out_weight.reshape(KV_HEADS, -1, width_out)
    gate_weight = field_codes(ffn_packed, 0, gate_scales)
    up_weight = field_codes(ffn_packed, 4, up_scales)
    down_weight = field_codes(ffn_packed.T, 8, down_scales)
    streams = []
    half_list = []
    for micro in range(micro_count):
        seq_lens = lax.dynamic_slice_in_dim(lengths[micro], first_row, seq_dev)
        attended = attend(
            queries[micro, 0],
            cache_keys[micro, 0],
            cache_values[micro, 0],
            new_keys[micro, 0],
            new_values[micro, 0],
            seq_lens,
            scale,
        )
        heads_all = lax.all_gather(attended, "head", axis=0, tiled=True)
        heads_all = heads_all.reshape(-1, KV_HEADS, seq_dev, heads_all.shape[1])
        projected = jnp.einsum(
            "sgie,gen->sin", heads_all, out_weight, preferred_element_type=jnp.float32
        )
        projected = projected.reshape(-1, width_out)
        stream = (residual[micro].astype(jnp.float32) + projected).astype(jnp.bfloat16)
        streams.append(stream)
        stream_f = stream.astype(jnp.float32)
        full_width = width_out * lax.axis_size("head")
        squares = lax.psum(jnp.sum(stream_f * stream_f, axis=1), "head")
        normed_part = (
            stream_f
            * lax.rsqrt(squares / full_width + epsilon)[:, None]
            * norm_gain.astype(jnp.float32)
        ).astype(jnp.bfloat16)
        gathered_rows = lax.all_gather(normed_part, "head", axis=1, tiled=True)
        half_rows = lax.all_to_all(gathered_rows, "batch", split_axis=1, concat_axis=0, tiled=True)
        half_list.append(half_rows)
    branches = []
    for half_rows in half_list:
        gate_part = jnp.dot(half_rows, gate_weight, preferred_element_type=jnp.float32)
        up_part = jnp.dot(half_rows, up_weight, preferred_element_type=jnp.float32)
        gate_sum, up_sum = (
            lax.psum(gate_part.astype(jnp.bfloat16), "batch").astype(jnp.float32),
            lax.psum(up_part.astype(jnp.bfloat16), "batch").astype(jnp.float32),
        )
        hidden = (jax.nn.silu(gate_sum) * up_sum).astype(jnp.bfloat16)
        partial_out = jnp.dot(hidden, down_weight, preferred_element_type=jnp.float32)
        branch = lax.psum_scatter(partial_out, "head", scatter_dimension=1, tiled=True)
        branches.append(branch.astype(jnp.bfloat16))
    branch_all = jnp.stack(branches)
    return (jnp.stack(streams), branch_all)


def solution(mesh):
    return jax.shard_map(
        body,
        mesh=mesh,
        in_specs=(
            P(None, ("replica", "batch"), "head"),
            P("head"),
            P(None, ("replica", "batch", "head"), None, None, None),
            P(None, ("replica", "batch", "head"), None, None, None),
            P(None, ("replica", "batch", "head"), None, None, None),
            P(None, ("replica", "batch", "head"), None, None),
            P(None, ("replica", "batch", "head"), None, None),
            P(None, "replica"),
            P(None, "head"),
            P(None, "head"),
            P("batch", "head"),
            P("batch", "head"),
            P("batch", "head"),
            P("head", "batch"),
        ),
        out_specs=(P(None, ("replica", "batch"), "head"), P(None, "replica", ("batch", "head"))),
        check_vma=False,
    )
```

profile of v0, /device:TPU:0, one launch (start us, length us, event | category | flops | bytes accessed | tf_op | source)
XLA Modules:
  0.0 627.9 jit_solution(5048884062242942342)
XLA Ops:
  7.2 0.8 fusion.72
  8.0 0.1 dynamic-slice_bitcast_fusion
  8.0 0.1 iota_compare_fusion
  8.1 0.7 slice_bitcast_fusion.1
  8.8 0.8 fusion.52
  9.6 1.2 select_reduce_fusion
  10.8 0.2 fusion.31
  11.0 0.7 bitcast_convert_fusion.1
  11.8 1.2 fusion.5
  12.9 32.3 %all-gather.1 = bf16[8,4,1024]{2,1,0:T(4,128)(2,1)S(1)} all-gather(bf16[1,4,1024]{2,1,0:T(4,128)(2,1)S(1)} %reshape.162), channel_id=1, replica_groups=mesh['replica'=2,'head'=8,'batch'=2] {'head'}, dimensions={0}, use_global_device_ids=true | all-gather | bytes 73728 | tf_op jit(solution)/shard_map/all_gather | solution.py:84
  45.2 17.5 %shift_right_arithmetic.40 = s32[4096,2,1024]{2,1,0:T(2,128)} broadcast(s32[4096,1024]{1,0:T(8,128)} %param.22), dimensions={0,2} | broadcast | bytes 50331648 | tf_op jit(solution)/shard_map/shift_right_arithmetic | solution.py:14
  62.7 39.9 %shift_right_arithmetic.41 = s32[8,1024,1024]{2,1,0:T(8,128)} reshape(s32[4096,2,1024]{2,1,0:T(2,128)} %shift_right_arithmetic.40) | data formatting | bytes 67108864 | tf_op jit(solution)/shard_map/shift_right_arithmetic | solution.py:14
  102.6 0.2 shift_right_arithmetic.43
  102.8 0.1 iota_compare_fusion.1
  102.8 0.3 select_reduce_fusion.1
  103.1 0.1 fusion.55
  103.2 0.2 fusion.30
  103.4 0.2 fusion.4
  103.7 30.5 %all-gather = bf16[8,4,1024]{2,1,0:T(4,128)(2,1)S(1)} all-gather(bf16[1,4,1024]{2,1,0:T(4,128)(2,1)S(1)} %reshape.160), channel_id=1, replica_groups=mesh['replica'=2,'head'=8,'batch'=2] {'head'}, dimensions={0}, use_global_device_ids=true | all-gather | bytes 73728 | tf_op jit(solution)/shard_map/all_gather | solution.py:84
  134.2 11.3 %broadcast_in_dim.61 = f32[64,128,1024]{2,1,0:T(8,128)} broadcast(bf16[64,1024]{1,0:T(8,128)(2,1)S(1)} %copy-done.4), dimensions={0,2} | broadcast | bytes 33685504 | tf_op jit(solution)/shard_map/broadcast_in_dim | solution.py:16
  145.4 27.5 %fusion.3 = bf16[8,1024,1024]{2,1,0:T(8,128)(2,1)} fusion(s32[8,1024,1024]{2,1,0:T(8,128)} %shift_right_arithmetic.41, s32[1024]{0:T(1024)S(1)} %shift_right_arithmetic.43, f32[8,1024,1024]{2,1,0:T(8,128)} %bitcast.132), kind=kLoop, calls=%fused_computation.7 | loop fusion | flops 50331648 | bytes 83890176 | tf_op jit(solution)/shard_map/convert_element_type | solution.py:17
  173.0 8.1 %fusion.73 = f32[4,1024,1]{1,0,2:T(4,128)S(1)} fusion(bf16[8,4,1024]{2,1,0:T(4,128)(2,1)S(1)} %all-gather.1, bf16[8,1024,1024]{2,1,0:T(8,128)(2,1)} %fusion.3), kind=kOutput, calls=%fused_computation.122 | convolution fusion | flops 67108864 | bytes 16859136 | tf_op jit(solution)/shard_map/sgie,gen->sin/dot_general | solution.py:86
  181.1 8.7 %fusion.32 = (bf16[1,4,1024]{2,1,0:T(4,128)(2,1)}, bf16[1,4,1024]{2,1,0:T(4,128)(2,1)}, f32[4,1024,1]{1,0,2:T(4,128)S(1)}) fusion(bf16[2,4,1024]{2,1,0:T(4,128)(2,1)S(1)} %copy-done.5, f32[4,1024,1]{1,0,2:T(4,128)S(1)} %fusion.73, bf16[8,4,1024]{2,1,0:T(4,128)(2,1)S(1)} %all-gather, bf16[8,1024,1024]{2,1,0:T(8,128)(2,1)} %fusion.3), kind=kOutput, calls=%fused_computation.60 | convolution fusion | flops 67133440 | bytes 16908288 | tf_op jit(solution)/shard_map/sgie,gen->sin/dot_general | solution.py:86
  189.7 0.2 fusion.38
  189.9 21.3 %all-reduce = (f32[4]{0:T(128)S(1)}, f32[4]{0:T(128)S(1)}) all-reduce(f32[4]{0:T(128)S(1)} %get-tuple-element.3, f32[4]{0:T(128)S(1)} %get-tuple-element.2), channel_id=1, replica_groups=mesh['replica'=2,'head'=8,'batch'=2] {'head'}, use_global_device_ids=true, to_apply=%region_10.11 | all-reduce | flops 8 | bytes 64 | tf_op jit(solution)/shard_map/psum | solution.py:94
  211.2 0.1 fusion.40
  211.3 32.5 %all_gather.15 = bf16[4,8192]{1,0:T(4,128)(2,1)} all-gather(bf16[4,1024]{1,0:T(4,128)(2,1)S(1)} %get-tuple-element.13), channel_id=1, replica_groups=mesh['replica'=2,'head'=8,'batch'=2] {'head'}, dimensions={1}, use_global_device_ids=true | all-gather | bytes 73728 | tf_op jit(solution)/shard_map/all_gather | solution.py:100
  243.8 3.3 all-to-all-start.1
  247.1 32.5 %all_gather.14 = bf16[4,8192]{1,0:T(4,128)(2,1)} all-gather(bf16[4,1024]{1,0:T(4,128)(2,1)S(1)} %get-tuple-element.12), channel_id=1, replica_groups=mesh['replica'=2,'head'=8,'batch'=2] {'head'}, dimensions={1}, use_global_device_ids=true | all-gather | bytes 73728 | tf_op jit(solution)/shard_map/all_gather | solution.py:100
  279.5 3.3 all-to-all-start
  282.9 0.2 all-reduce.4.cloned.1.call-start
  283.2 45.7 %fusion.2 = (bf16[4096,4096]{1,0:T(8,128)(2,1)}, bf16[4096,4096]{1,0:T(8,128)(2,1)}) fusion(s32[4096,4096]{1,0:T(8,128)} %param.24, f32[32,4096]{1,0:T(8,128)S(1)} %convert_element_type.191, f32[32,4096]{1,0:T(8,128)S(1)} %convert_element_type.196), kind=kLoop, calls=%fused_computation.5 | loop fusion | flops 201326592 | bytes 135266304 | tf_op jit(solution)/shard_map/convert_element_type | solution.py:23
  328.9 13.4 %convolution_convert_fusion = bf16[8,4096]{1,0:T(8,128)(2,1)} fusion(bf16[8,4096]{1,0:T(8,128)(2,1)S(1)} %all_to_all.35, bf16[4096,4096]{1,0:T(8,128)(2,1)} %get-tuple-element.11), kind=kOutput, calls=%fused_computation.8 | convolution fusion | flops 268468224 | bytes 33685504 | tf_op jit(solution)/shard_map/dot_general | solution.py:106
  342.4 13.4 %convolution_convert_fusion.1 = bf16[8,4096]{1,0:T(8,128)(2,1)} fusion(bf16[8,4096]{1,0:T(8,128)(2,1)S(1)} %all_to_all.35, bf16[4096,4096]{1,0:T(8,128)(2,1)} %get-tuple-element.10), kind=kOutput, calls=%fused_computation.9 | convolution fusion | flops 268468224 | bytes 33685504 | tf_op jit(solution)/shard_map/dot_general | solution.py:105
  355.8 13.5 %convolution_convert_fusion.2 = bf16[8,4096]{1,0:T(8,128)(2,1)} fusion(bf16[8,4096]{1,0:T(8,128)(2,1)S(1)} %all_to_all.31, bf16[4096,4096]{1,0:T(8,128)(2,1)} %get-tuple-element.11), kind=kOutput, calls=%fused_computation.10 | convolution fusion | flops 268468224 | bytes 33685504 | tf_op jit(solution)/shard_map/dot_general | solution.py:106
  369.3 13.4 %convolution_convert_fusion.3 = bf16[8,4096]{1,0:T(8,128)(2,1)} fusion(bf16[8,4096]{1,0:T(8,128)(2,1)S(1)} %all_to_all.31, bf16[4096,4096]{1,0:T(8,128)(2,1)} %get-tuple-element.10), kind=kOutput, calls=%fused_computation.11 | convolution fusion | flops 268468224 | bytes 33685504 | tf_op jit(solution)/shard_map/dot_general | solution.py:105
  382.8 0.3 reduce-scatter.3.cloned.1.call-start
  383.1 0.3 copy.21
  383.4 41.1 %broadcast_in_dim.65 = f32[32,128,4096]{1,0,2:T(8,128)} broadcast(f32[32,4096]{0,1:T(8,128)S(1)} %copy.21), dimensions={0,2} | broadcast | bytes 67633152 | tf_op jit(solution)/shard_map/broadcast_in_dim | solution.py:22
  424.5 58.4 %fusion = bf16[4096,4096]{0,1:T(8,128)(2,1)} fusion(f32[512,8,32,128]{3,2,1,0:T(8,128)} %bitcast.39, s32[4096,4096]{1,0:T(8,128)} %param.24), kind=kLoop, calls=%fused_computation.1 | loop fusion | flops 100663296 | bytes 167772160 | tf_op jit(solution)/shard_map/convert_element_type | solution.py:23
  483.0 15.2 %fusion.24 = f32[8,4096]{1,0:T(8,128)} fusion(bf16[4096,4096]{0,1:T(8,128)(2,1)} %fusion, bf16[8,4096]{1,0:T(8,128)(2,1)} %get-tuple-element.8, bf16[8,4096]{1,0:T(8,128)(2,1)} %get-tuple-element.9), kind=kOutput, calls=%fused_computation.40 | convolution fusion | flops 268697600 | bytes 33816576 | tf_op jit(solution)/shard_map/dot_general | solution.py:112
  498.2 15.2 %fusion.26 = f32[8,4096]{1,0:T(8,128)} fusion(bf16[4096,4096]{0,1:T(8,128)(2,1)} %fusion, bf16[8,4096]{1,0:T(8,128)(2,1)S(1)} %copy-done.6, bf16[8,4096]{1,0:T(8,128)(2,1)S(1)} %copy-done.7), kind=kOutput, calls=%fused_computation.41 | convolution fusion | flops 268697600 | bytes 33816576 | tf_op jit(solution)/shard_map/dot_general | solution.py:112
  513.4 0.6 pad_maximum_fusion
  514.0 42.4 %reduce-scatter.3.cloned.1.call-done = f32[8,512]{1,0:T(8,128)} async-done(((f32[8,4096]{1,0:T(8,128)}), f32[8,512]{1,0:T(8,128)}) %reduce-scatter.3.cloned.1.call-update) | async-done | bytes 16400 | tf_op jit(solution)/shard_map/reduce_scatter | solution.py:113
  556.5 0.7 convert_bitcast_fusion.3
  557.2 62.9 %reduce-scatter.5.cloned.1.call-done = f32[8,512]{1,0:T(8,128)} async-done(((f32[8,4096]{1,0:T(8,128)}), f32[8,512]{1,0:T(8,128)}) %reduce-scatter.5.cloned.1.call-update) | async-done | bytes 16400 | tf_op jit(solution)/shard_map/reduce_scatter | solution.py:113
  620.1 0.7 convert_bitcast_fusion.2
  620.8 0.6 pad_maximum_fusion.1
  (48 shorter events, 0.4 us)
Async XLA Ops:
  62.7 40.2 %copy-start = (bf16[2,1,4,256,128]{4,3,2,1,0:T(8,128)(2,1)S(1)}, bf16[2,1,4,256,128]{4,3,2,1,0:T(8,128)(2,1)}, u32[]{:S(2)}) copy-start(bf16[2,1,4,256,128]{4,3,2,1,0:T(8,128)(2,1)} %param.17) | copy-start | bytes 1572868
  62.7 40.2 %copy-start.10 = (bf16[2,1,4,8,128]{4,3,2,1,0:T(8,128)(2,1)S(1)}, bf16[2,1,4,8,128]{4,3,2,1,0:T(8,128)(2,1)}, u32[]{:S(2)}) copy-start(bf16[2,1,4,8,128]{4,3,2,1,0:T(8,128)(2,1)} %param.16) | copy-start | bytes 49156
  62.7 40.7 %copy-start.12 = (bf16[2,1,4,256,128]{4,3,2,1,0:T(8,128)(2,1)S(1)}, bf16[2,1,4,256,128]{4,3,2,1,0:T(8,128)(2,1)}, u32[]{:S(2)}) copy-start(bf16[2,1,4,256,128]{4,3,2,1,0:T(8,128)(2,1)} %param.18) | copy-start | bytes 1572868
  62.7 71.5 %copy-start.4 = (bf16[64,1024]{1,0:T(8,128)(2,1)S(1)}, bf16[64,1024]{1,0:T(8,128)(2,1)}, u32[]{:S(2)}) copy-start(bf16[64,1024]{1,0:T(8,128)(2,1)} %param.23) | copy-start | bytes 393220
  145.4 35.6 %copy-start.5 = (bf16[2,4,1024]{2,1,0:T(4,128)(2,1)S(1)}, bf16[2,4,1024]{2,1,0:T(4,128)(2,1)}, u32[]{:S(2)}) copy-start(bf16[2,4,1024]{2,1,0:T(4,128)(2,1)} %param.14) | copy-start | bytes 49156
  173.0 38.2 %copy-start.11 = (bf16[1024]{0:T(1024)(128)(2,1)S(1)}, bf16[1024]{0:T(1024)(128)(2,1)}, u32[]{:S(2)}) copy-start(bf16[1024]{0:T(1024)(128)(2,1)} %param.15) | copy-start | bytes 6148
  173.0 110.1 %copy-start.1 = (bf16[32,4096]{1,0:T(8,128)(2,1)S(1)}, bf16[32,4096]{1,0:T(8,128)(2,1)}, u32[]{:S(2)}) copy-start(bf16[32,4096]{1,0:T(8,128)(2,1)} %param.25) | copy-start | bytes 786436
  173.0 110.2 %copy-start.2 = (bf16[32,4096]{1,0:T(8,128)(2,1)S(1)}, bf16[32,4096]{1,0:T(8,128)(2,1)}, u32[]{:S(2)}) copy-start(bf16[32,4096]{1,0:T(8,128)(2,1)} %param.26) | copy-start | bytes 786436
  243.8 35.8 %all-to-all-start.1 = ((bf16[4,2,4096]{2,0,1:T(4,128)(2,1)}), bf16[4,2,4096]{2,0,1:T(4,128)(2,1)S(1)}, u32[]{:S(2)}, u32[]{:S(2)}) async-start(bf16[4,2,4096]{2,0,1:T(4,128)(2,1)} %bitcast.31), calls=%async_computation.2 | async-start | bytes 131072 | tf_op jit(solution)/shard_map/all_to_all | solution.py:101
  279.5 76.3 %all-to-all-start = ((bf16[4,2,4096]{2,0,1:T(4,128)(2,1)}), bf16[4,2,4096]{2,0,1:T(4,128)(2,1)S(1)}, u32[]{:S(2)}, u32[]{:S(2)}) async-start(bf16[4,2,4096]{2,0,1:T(4,128)(2,1)} %bitcast.24), calls=%async_computation | async-start | bytes 131072 | tf_op jit(solution)/shard_map/all_to_all | solution.py:101
  282.9 200.1 %all-reduce.4.cloned.1.call-start = ((), (), s32[]{:S(2)}) async-start(), calls=%async_computation.6 | async-start | bytes 524288 | tf_op jit(solution)/shard_map/psum | solution.py:109
  355.8 27.2 %copy-start.3 = (bf16[32,4096]{1,0:T(8,128)(2,1)S(1)}, bf16[32,4096]{1,0:T(8,128)(2,1)}, u32[]{:S(2)}) copy-start(bf16[32,4096]{1,0:T(8,128)(2,1)} %param.27) | copy-start | bytes 786436
  382.8 173.7 %reduce-scatter.3.cloned.1.call-start = ((), (), s32[]{:S(2)}) async-start(), calls=%async_computation.4 | async-start | bytes 147456 | tf_op jit(solution)/shard_map/reduce_scatter | solution.py:113
  482.9 15.3 %copy-start.6 = (bf16[8,4096]{1,0:T(8,128)(2,1)S(1)}, bf16[8,4096]{1,0:T(8,128)(2,1)}, u32[]{:S(2)}) copy-start(bf16[8,4096]{1,0:T(8,128)(2,1)} %get-tuple-element.6) | copy-start | bytes 196612
  482.9 15.3 %copy-start.7 = (bf16[8,4096]{1,0:T(8,128)(2,1)S(1)}, bf16[8,4096]{1,0:T(8,128)(2,1)}, u32[]{:S(2)}) copy-start(bf16[8,4096]{1,0:T(8,128)(2,1)} %get-tuple-element.7) | copy-start | bytes 196612
  482.9 30.5 %copy-start.8 = (bf16[1,4,1024]{2,1,0:T(4,128)(2,1)S(1)}, bf16[1,4,1024]{2,1,0:T(4,128)(2,1)}, u32[]{:S(2)}) copy-start(bf16[1,4,1024]{2,1,0:T(4,128)(2,1)} %get-tuple-element.14) | copy-start | bytes 24580
  482.9 30.5 %copy-start.9 = (bf16[1,4,1024]{2,1,0:T(4,128)(2,1)S(1)}, bf16[1,4,1024]{2,1,0:T(4,128)(2,1)}, u32[]{:S(2)}) copy-start(bf16[1,4,1024]{2,1,0:T(4,128)(2,1)} %get-tuple-element.15) | copy-start | bytes 24580
  498.1 121.9 %reduce-scatter.5.cloned.1.call-start = ((), (), s32[]{:S(2)}) async-start(), calls=%async_computation.5 | async-start | bytes 147456 | tf_op jit(solution)/shard_map/reduce_scatter | solution.py:113
Sparse Core Ops, SparseCore 0:
  382.9 15.7 all-reduce.3
  498.3 58.1 reduce-scatter.2
  560.1 59.8 reduce-scatter.4
where the time goes:
time: 630 us; the launch traced here: 628 us
  blocking collectives  149 us (24%)
  other arithmetic  136 us (22%)
  local copies, waits for them, and re-layouts  112 us (18%)
  matrix products  105 us (17%)
  waiting for transfers between devices  105 us (17%)
  between operations  14 us (2%)
  starting transfers between devices  7.12 us (1%)
    reduce_scatter x2, waiting for transfers between devices, body(): lax.psum_scatter(partial_out, 'head', scatter_dimension=1, tiled=True)  105 us
    convert_element_type x2, other arithmetic, field_codes(): return (nibbles * spread).astype(jnp.bfloat16)  104 us
    all_gather x2, blocking collectives, body(): gathered_rows = lax.all_gather(normed_part, 'head', axis=1, tiled=True)  65 us
    all_gather x2, blocking collectives, body(): heads_all = lax.all_gather(attended, 'head', axis=0, tiled=True)  62.8 us
    shift_right_arithmetic x4, local copies, waits for them, and re-layouts, unpack_pairs(): jnp.right_shift(packed[:, None, :], shifts[None, :, None])  57.5 us
    broadcast_in_dim x1, local copies, waits for them, and re-layouts, field_codes(): jnp.repeat(scales.astype(jnp.float32), words.shape[0] // scales.shape[0],...  41.1 us
    dot_general x2, matrix products, body(): jnp.dot(hidden, down_weight, preferred_element_type=jnp.float32)  30.3 us
    convert_element_type x1, other arithmetic, unpack_pairs(): return (nibbles * spread).astype(jnp.bfloat16)  27.5 us
  transfers between devices with their start and end apart: 5, of which 2 were waited for; matrix products, arithmetic and copies ran while one was open for 30% of the time, Pallas kernels for 0%

commit v1 on v0

v1 whole, which is shorter than its diff:
```python
import functools

import jax
import jax.numpy as jnp
from jax import lax
from jax.experimental import pallas as pl
from jax.experimental.pallas import tpu as pltpu
from jax.sharding import PartitionSpec as P

KV_HEADS = 8
GROUP = 128
EPSILON = 1e-05
MESH = pl.DeviceIdType.MESH
F32 = jnp.float32
BF16 = jnp.bfloat16
CHUNK = 256
FTILE = 512
NT = (((1,), (1,)), ((), ()))


def kernel(
    heads,
    blocks,
    res_ref,
    gain_ref,
    q_ref,
    ck_ref,
    cv_ref,
    nk_ref,
    nv_ref,
    len_ref,
    op_ref,
    os_ref,
    fp_ref,
    gs_ref,
    us_ref,
    ds_ref,
    stream_ref,
    out_ref,
    oring,
    ocodes,
    osf,
    gsf,
    usf,
    dsf,
    mix,
    att_mine,
    att_all,
    att_lhs,
    x_mine,
    x_all,
    sq_mine,
    sq_all,
    nbd,
    nsum,
    fring,
    dcodes,
    acc,
    part_send,
    part_recv,
    acc_out,
    rs_send,
    rs_recv,
    osem,
    fsem,
    att_ss,
    att_rs,
    x_ss,
    x_rs,
    sq_ss,
    sq_rs,
    pt_ss,
    pt_rs,
    rd_ss,
    rd_rs,
):
    head = lax.axis_index("head")
    batch = lax.axis_index("batch")
    half = heads // 2
    inst = q_ref.shape[0]
    qper = q_ref.shape[1]
    positions = ck_ref.shape[1]
    rows = res_ref.shape[0]
    width = res_ref.shape[1]
    both = 2 * rows
    feat = fp_ref.shape[0]
    hidden_units = fp_ref.shape[1]
    words = op_ref.shape[0]
    out_slots = oring.shape[0]
    ffn_slots = fring.shape[0]
    out_chunks = words // CHUNK
    kchunks = feat // CHUNK
    ftiles = hidden_units // FTILE
    total_chunks = kchunks * ftiles

    def out_copy(c):
        slot = lax.rem(c, out_slots)
        first = pl.multiple_of(c * CHUNK, CHUNK)
        return pltpu.make_async_copy(
            op_ref.at[pl.ds(first, CHUNK), :], oring.at[slot], osem.at[slot]
        )

    def ffn_copy(c):
        slot = lax.rem(c, ffn_slots)
        j = c // kchunks
        k = lax.rem(c, kchunks)
        return pltpu.make_async_copy(
            fp_ref.at[
                pl.ds(pl.multiple_of(k * CHUNK, CHUNK), CHUNK),
                pl.ds(pl.multiple_of(j * FTILE, FTILE), FTILE),
            ],
            fring.at[slot],
            fsem.at[slot],
        )

    def start_out(c, _):
        out_copy(c).start()
        return 0

    def start_ffn(c, _):
        ffn_copy(c).start()
        return 0

    barrier = pltpu.get_barrier_semaphore()

    def greet(i, _):
        other = lax.rem(head + i, heads)
        pl.semaphore_signal(
            barrier, inc=1, device_id={"head": other, "batch": 1 - batch}, device_id_type=MESH
        )

        @pl.when(i > 0)
        def _():
            pl.semaphore_signal(
                barrier, inc=1, device_id={"head": other, "batch": batch}, device_id_type=MESH
            )

        return 0

    lax.fori_loop(0, heads, greet, 0)
    lax.fori_loop(0, out_slots, start_out, 0)
    lax.fori_loop(0, ffn_slots, start_ffn, 0)

    scale = q_ref.shape[2] ** (-0.5)
    new_k = nk_ref[...].astype(F32)
    new_v = nv_ref[...].astype(F32)
    where = lax.broadcasted_iota(jnp.int32, (qper, positions), 1)
    for i in range(inst):
        q = q_ref[i]
        scores = lax.dot_general(q, ck_ref[i], NT, preferred_element_type=F32) * scale
        live = where < len_ref[i : i + 1, :]
        scores = jnp.where(live, scores, -jnp.inf)
        score_new = jnp.sum(q.astype(F32) * new_k[i : i + 1, :], axis=1, keepdims=True) * scale
        top = jnp.maximum(jnp.max(scores, axis=1, keepdims=True), score_new)
        weights = jnp.where(live, jnp.exp(scores - top), 0.0)
        weight_new = jnp.exp(score_new - top)
        total = jnp.sum(weights, axis=1, keepdims=True) + weight_new
        probs = (weights / total).astype(BF16)
        prob_new = (weight_new / total).astype(BF16).astype(F32)
        mixed = jnp.dot(probs, cv_ref[i], preferred_element_type=F32)
        mix[i] = mixed + prob_new * new_v[i : i + 1, :]
    e = lax.broadcasted_iota(jnp.int32, (GROUP, GROUP), 0)
    c = lax.broadcasted_iota(jnp.int32, (GROUP, GROUP), 1)
    from_e = jnp.where(c < GROUP // 2, 2 * c, 2 * c - GROUP + 1)
    perm = jnp.where(e == from_e, 1.0, 0.0).astype(BF16)
    hq = qper // 2
    for k in range(hq):
        lo = jnp.dot(mix[:, k, :].astype(BF16), perm, preferred_element_type=F32)
        hi = jnp.dot(mix[:, hq + k, :].astype(BF16), perm, preferred_element_type=F32)
        att_mine[:, k * GROUP : (k + 1) * GROUP] = jnp.concatenate([lo, hi], axis=0).astype(BF16)

    pl.semaphore_wait(barrier, 2 * heads - 1)

    def att_copy(i):
        other = lax.rem(head + i, heads)
        return pltpu.make_async_remote_copy(
            src_ref=att_mine,
            dst_ref=att_all.at[head],
            send_sem=att_ss.at[i],
            recv_sem=att_rs.at[head],
            device_id={"head": other, "batch": batch},
            device_id_type=MESH,
        )

    def att_arrival(i):
        other = lax.rem(head + i, heads)
        return pltpu.make_async_remote_copy(
            src_ref=att_mine,
            dst_ref=att_all.at[other],
            send_sem=att_ss.at[i],
            recv_sem=att_rs.at[other],
            device_id={"head": other, "batch": batch},
            device_id_type=MESH,
        )

    def att_start(i, _):
        att_copy(i).start()
        return 0

    lax.fori_loop(1, heads, att_start, 0)
    att_all[head] = att_mine[...]

    osf[...] = os_ref[...].astype(F32)
    gsf[...] = gs_ref[...].astype(F32)
    usf[...] = us_ref[...].astype(F32)
    dsf[...] = ds_ref[...].astype(F32)
    hg = GROUP // 2

    def out_unpack(c, _):
        out_copy(c).wait()
        slot = lax.rem(c, out_slots)
        for s in range(CHUNK // hg):
            w = oring[slot, s * hg : (s + 1) * hg, :]
            g = c * (CHUNK // hg) + s
            ocodes[g, 0:hg, :] = (w & 15).astype(F32).astype(BF16)
            ocodes[g, hg:GROUP, :] = (w >> 4).astype(F32).astype(BF16)

        @pl.when(c + out_slots < out_chunks)
        def _():
            out_copy(c + out_slots).start()

        return 0

    lax.fori_loop(0, out_chunks, out_unpack, 0)

    def att_wait(i, _):
        att_copy(i).wait_send()
        att_arrival(i).wait_recv()
        return 0

    lax.fori_loop(1, heads, att_wait, 0)

    for unit in range(heads):
        block, g = unit // KV_HEADS, unit % KV_HEADS
        tile = att_all[unit].astype(F32)
        for k in range(qper):
            part = tile[(k // hq) * inst : (k // hq + 1) * inst, (k % hq) * GROUP : (k % hq + 1) * GROUP]
            att_lhs[g * qper + k, block * inst : (block + 1) * inst, :] = part

    def project(gg, total):
        for s in range(2):
            g = gg * 2 + s
            lhs = att_lhs[g]
            p = jnp.dot(lhs.astype(BF16), ocodes[g], preferred_element_type=F32)
            corr = 8.0 * jnp.sum(lhs, axis=1, keepdims=True)
            total = total + osf[pl.ds(g, 1), :] * (p - corr)
        return total

    projected = lax.fori_loop(0, 2 * words // GROUP // 2, project, jnp.zeros((rows, width), F32))
    stream = (res_ref[...] + projected).astype(BF16)
    stream_ref[...] = stream
    stream_f = stream.astype(F32)
    sq_mine[...] = jnp.broadcast_to(
        jnp.sum(stream_f * stream_f, axis=1, keepdims=True), sq_mine.shape
    )
    x_mine[...] = stream_f * gain_ref[...]

    owner = head // half
    place = batch * half + lax.rem(head, half)

    def x_copy(i):
        other = lax.rem(head + i, heads)
        return pltpu.make_async_remote_copy(
            src_ref=x_mine,
            dst_ref=x_all.at[place],
            send_sem=x_ss.at[i],
            recv_sem=x_rs.at[place],
            device_id={"head": other, "batch": owner},
            device_id_type=MESH,
        )

    def sq_copy(i):
        other = lax.rem(head + i // 2, heads)
        other_b = lax.rem(batch + i, 2)
        return pltpu.make_async_remote_copy(
            src_ref=sq_mine,
            dst_ref=sq_all.at[batch * heads + head],
            send_sem=sq_ss.at[i],
            recv_sem=sq_rs.at[batch * heads + head],
            device_id={"head": other, "batch": other_b},
            device_id_type=MESH,
        )

    def x_start(i, _):
        @pl.when(jnp.logical_or(i > 0, owner != batch))
        def _():
            x_copy(i).start()

        return 0

    def sq_start(i, _):
        sq_copy(i).start()
        return 0

    lax.fori_loop(0, heads, x_start, 0)
    lax.fori_loop(1, 2 * heads, sq_start, 0)

    @pl.when(owner == batch)
    def _():
        x_all[place] = x_mine[...]

    sq_all[batch * heads + head] = sq_mine[...]

    def x_wait_send(i, _):
        @pl.when(jnp.logical_or(i > 0, owner != batch))
        def _():
            x_copy(i).wait_send()

        return 0

    def x_wait(p, _):
        @pl.when(jnp.logical_or(p != place, owner != batch))
        def _():
            pltpu.make_async_remote_copy(
                src_ref=x_mine,
                dst_ref=x_all.at[p],
                send_sem=x_ss.at[0],
                recv_sem=x_rs.at[p],
                device_id={"head": head, "batch": 1 - batch},
                device_id_type=MESH,
            ).wait_recv()

        return 0

    def sq_wait_send(i, _):
        sq_copy(i).wait_send()
        return 0

    def sq_wait(p, _):
        @pl.when(p != batch * heads + head)
        def _():
            pltpu.make_async_remote_copy(
                src_ref=sq_mine,
                dst_ref=sq_all.at[p],
                send_sem=sq_ss.at[0],
                recv_sem=sq_rs.at[p],
                device_id={"head": head, "batch": 1 - batch},
                device_id_type=MESH,
            ).wait_recv()

        return 0

    lax.fori_loop(0, heads, x_wait_send, 0)
    lax.fori_loop(1, 2 * heads, sq_wait_send, 0)
    lax.fori_loop(0, heads, x_wait, 0)
    lax.fori_loop(0, 2 * heads, sq_wait, 0)

    roots = []
    for b in range(2):
        squares = sq_all[b * heads]
        for h in range(1, heads):
            squares = squares + sq_all[b * heads + h]
        roots.append(lax.rsqrt(squares / (width * heads) + EPSILON))
    zeros = jnp.zeros((both, GROUP), BF16)
    for g in range(feat // GROUP):
        hh, off = g * GROUP // width, g * GROUP % width
        pieces = [x_all[b * half + hh, :, off : off + GROUP] * roots[b] for b in range(2)]
        x = jnp.concatenate(pieces, axis=0).astype(BF16)
        kp, odd = g // 2, g % 2
        lanes = slice(odd * GROUP, (odd + 1) * GROUP)
        nbd[kp, odd * both : (odd + 1) * both, lanes] = x
        nbd[kp, (1 - odd) * both : (2 - odd) * both, lanes] = zeros
        nsum[g] = jnp.broadcast_to(
            8.0 * jnp.sum(x.astype(F32), axis=1, keepdims=True), (both, GROUP)
        )

    acc_out[...] = jnp.zeros_like(acc_out)

    def part_copy(j):
        return pltpu.make_async_remote_copy(
            src_ref=part_send.at[j],
            dst_ref=part_recv.at[j],
            send_sem=pt_ss.at[j],
            recv_sem=pt_rs.at[j],
            device_id={"head": head, "batch": 1 - batch},
            device_id_type=MESH,
        )

    def down(j):
        slot = lax.rem(j, 2)
        part_copy(j).wait()
        gate = acc[slot, 0] + part_recv[j, 0].astype(F32)
        up = acc[slot, 1] + part_recv[j, 1].astype(F32)
        hidden = (gate / (1.0 + jnp.exp(-gate)) * up).astype(BF16)
        lhs, corr = [], []
        for pp in range(FTILE // 256):
            h0 = hidden[:, pp * 256 : pp * 256 + GROUP]
            h1 = hidden[:, pp * 256 + GROUP : (pp + 1) * 256]
            lhs.append(
                jnp.concatenate(
                    [jnp.concatenate([h0, zeros], axis=1), jnp.concatenate([zeros, h1], axis=1)],
                    axis=0,
                )
            )
            for h in (h0, h1):
                corr.append(8.0 * jnp.sum(h.astype(F32), axis=1, keepdims=True))

        def dchunk(n, _):
            first = pl.multiple_of(n * CHUNK, CHUNK)
            total = acc_out[:, pl.ds(first, CHUNK)]
            for pp in range(FTILE // 256):
                codes = dcodes[slot, pl.ds(first, CHUNK), pp * 256 : (pp + 1) * 256]
                p = lax.dot_general(lhs[pp], codes, NT, preferred_element_type=F32)
                for s in range(2):
                    g = j * (FTILE // GROUP) + pp * 2 + s
                    row = dsf[pl.ds(g, 1), pl.ds(first, CHUNK)]
                    total = total + row * (p[s * both : (s + 1) * both] - corr[pp * 2 + s])
            acc_out[:, pl.ds(first, CHUNK)] = total
            return 0

        lax.fori_loop(0, feat // CHUNK, dchunk, 0)

    def ftile(j, _):
        slot = lax.rem(j, 2)
        acc[slot] = jnp.zeros(acc.shape[1:], F32)

        def chunk(k, _):
            c = j * kchunks + k
            rslot = lax.rem(c, ffn_slots)
            ffn_copy(c).wait()
            lhs = nbd[k]
            n0 = jnp.concatenate([nsum[2 * k]] * 2, axis=1)
            n1 = jnp.concatenate([nsum[2 * k + 1]] * 2, axis=1)
            for n in range(FTILE // 256):
                cols = slice(n * 256, (n + 1) * 256)
                w = fring[rslot, :, cols]
                at = pl.ds(pl.multiple_of(j * FTILE + n * 256, 256), 256)
                dcodes[slot, pl.ds(pl.multiple_of(k * CHUNK, CHUNK), CHUNK), cols] = (
                    (w >> 8).astype(F32).astype(BF16)
                )
                for which, scales in ((0, gsf), (1, usf)):
                    bits = (w & 15) if which == 0 else ((w >> 4) & 15)
                    p = jnp.dot(lhs, bits.astype(F32).astype(BF16), preferred_element_type=F32)
                    acc[slot, which, :, cols] += (
                        scales[pl.ds(2 * k, 1), at] * (p[:both] - n0)
                        + scales[pl.ds(2 * k + 1, 1), at] * (p[both:] - n1)
                    )

            @pl.when(c + ffn_slots < total_chunks)
            def _():
                ffn_copy(c + ffn_slots).start()

            return 0

        lax.fori_loop(0, kchunks, chunk, 0)
        part_send[j] = acc[slot].astype(BF16)
        part_copy(j).start()

        @pl.when(j > 0)
        def _():
            down(j - 1)

        return 0

    lax.fori_loop(0, ftiles, ftile, 0)
    down(ftiles - 1)

    share = out_ref.shape[1]
    for t in range(heads):
        rs_send[t] = acc_out[:, t * share : (t + 1) * share].astype(BF16)

    def rs_copy(i):
        other = lax.rem(head + i, heads)
        return pltpu.make_async_remote_copy(
            src_ref=rs_send.at[other],
            dst_ref=rs_recv.at[head],
            send_sem=rd_ss.at[i],
            recv_sem=rd_rs.at[head],
            device_id={"head": other, "batch": batch},
            device_id_type=MESH,
        )

    def rs_start(i, _):
        rs_copy(i).start()
        return 0

    lax.fori_loop(1, heads, rs_start, 0)
    rs_recv[head] = rs_send[head]

    def rs_wait(i, _):
        other = lax.rem(head + i, heads)
        rs_copy(i).wait_send()
        pltpu.make_async_remote_copy(
            src_ref=rs_send.at[other],
            dst_ref=rs_recv.at[other],
            send_sem=rd_ss.at[i],
            recv_sem=rd_rs.at[other],
            device_id={"head": other, "batch": batch},
            device_id_type=MESH,
        ).wait_recv()
        return 0

    lax.fori_loop(1, heads, rs_wait, 0)
    result = rs_recv[0].astype(F32)
    for t in range(1, heads):
        result = result + rs_recv[t].astype(F32)
    out_ref[...] = result.astype(BF16)


def body(
    residual,
    norm_gain,
    queries,
    cache_keys,
    cache_values,
    new_keys,
    new_values,
    lengths,
    out_packed,
    out_scales,
    ffn_packed,
    gate_scales,
    up_scales,
    down_scales,
):
    micro, _, slots, qper, hd = queries.shape
    heads = lax.axis_size("head")
    positions = cache_keys.shape[3]
    inst = micro * slots
    blocks = residual.shape[1] // slots
    rows = micro * residual.shape[1]
    width = residual.shape[2]
    feat, hidden_units = ffn_packed.shape
    words = out_packed.shape[0]
    both = 2 * rows
    share = feat // heads
    ftiles = hidden_units // FTILE
    unit = lax.axis_index("batch") * heads + lax.axis_index("head")
    first_row = unit // KV_HEADS * slots
    lens = lax.dynamic_slice_in_dim(lengths, first_row, slots, axis=1).reshape(inst, 1)
    lens = jnp.broadcast_to(lens, (inst, positions))
    res = residual.reshape(micro, blocks, slots, width).transpose(1, 0, 2, 3)
    res = res.reshape(rows, width).astype(F32)
    gain = norm_gain.astype(F32).reshape(1, width)
    out_slots = min(8, words // CHUNK)
    ffn_slots = min(16, (feat // CHUNK) * ftiles)
    groups = 2 * words // GROUP
    vmem = pl.BlockSpec(memory_space=pltpu.VMEM)
    anywhere = pl.BlockSpec(memory_space=pl.ANY)
    dma = pltpu.SemaphoreType.DMA
    stream, out = pl.pallas_call(
        functools.partial(kernel, heads, blocks),
        out_shape=(
            jax.ShapeDtypeStruct((rows, width), BF16),
            jax.ShapeDtypeStruct((both, share), BF16),
        ),
        in_specs=[vmem] * 8 + [anywhere, vmem, anywhere, vmem, vmem, vmem],
        out_specs=(vmem, vmem),
        scratch_shapes=[
            pltpu.VMEM((out_slots, CHUNK, width), jnp.int32),
            pltpu.VMEM((groups, GROUP, width), BF16),
            pltpu.VMEM(out_scales.shape, F32),
            pltpu.VMEM(gate_scales.shape, F32),
            pltpu.VMEM(up_scales.shape, F32),
            pltpu.VMEM(down_scales.shape, F32),
            pltpu.VMEM((inst, qper, hd), F32),
            pltpu.VMEM((2 * inst, qper // 2 * hd), BF16),
            pltpu.VMEM((heads, 2 * inst, qper // 2 * hd), BF16),
            pltpu.VMEM((groups, rows, GROUP), F32),
            pltpu.VMEM((rows, width), F32),
            pltpu.VMEM((heads, rows, width), F32),
            pltpu.VMEM((rows, GROUP), F32),
            pltpu.VMEM((2 * heads, rows, GROUP), F32),
            pltpu.VMEM((feat // 256, 2 * both, 256), BF16),
            pltpu.VMEM((feat // GROUP, both, GROUP), F32),
            pltpu.VMEM((ffn_slots, CHUNK, FTILE), jnp.int32),
            pltpu.VMEM((2, feat, FTILE), BF16),
            pltpu.VMEM((2, 2, both, FTILE), F32),
            pltpu.VMEM((ftiles, 2, both, FTILE), BF16),
            pltpu.VMEM((ftiles, 2, both, FTILE), BF16),
            pltpu.VMEM((both, feat), F32),
            pltpu.VMEM((heads, both, share), BF16),
            pltpu.VMEM((heads, both, share), BF16),
            dma((out_slots,)),
            dma((ffn_slots,)),
            dma((heads,)),
            dma((heads,)),
            dma((heads,)),
            dma((heads,)),
            dma((2 * heads,)),
            dma((2 * heads,)),
            dma((ftiles,)),
            dma((ftiles,)),
            dma((heads,)),
            dma((heads,)),
        ],
        compiler_params=pltpu.CompilerParams(
            collective_id=0, has_side_effects=True, vmem_limit_bytes=58 * 1024 * 1024
        ),
    )(
        res,
        gain,
        queries.reshape(inst, qper, hd),
        cache_keys.reshape(inst, positions, hd),
        cache_values.reshape(inst, positions, hd),
        new_keys.reshape(inst, hd),
        new_values.reshape(inst, hd),
        lens,
        out_packed,
        out_scales,
        ffn_packed,
        gate_scales,
        up_scales,
        down_scales,
    )
    stream = stream.reshape(blocks, micro, slots, width).transpose(1, 0, 2, 3)
    stream = stream.reshape(micro, blocks * slots, width)
    out = out.reshape(2, blocks, micro, slots, share).transpose(2, 0, 1, 3, 4)
    out = out.reshape(micro, 2 * blocks * slots, share)
    return (stream, out)


def solution(mesh):
    return jax.shard_map(
        body,
        mesh=mesh,
        in_specs=(
            P(None, ("replica", "batch"), "head"),
            P("head"),
            P(None, ("replica", "batch", "head"), None, None, None),
            P(None, ("replica", "batch", "head"), None, None, None),
            P(None, ("replica", "batch", "head"), None, None, None),
            P(None, ("replica", "batch", "head"), None, None),
            P(None, ("replica", "batch", "head"), None, None),
            P(None, "replica"),
            P(None, "head"),
            P(None, "head"),
            P("batch", "head"),
            P("batch", "head"),
            P("batch", "head"),
            P("head", "batch"),
        ),
        out_specs=(P(None, ("replica", "batch"), "head"), P(None, "replica", ("batch", "head"))),
        check_vma=False,
    )
```

time: 630 us -> 104 us (0.17)
  blocking collectives: 149 us -> 0 us
  other arithmetic: 136 us -> 1.27 us
  local copies, waits for them, and re-layouts: 112 us -> 5.49 us
  matrix products: 105 us -> 0 us
  waiting for transfers between devices: 105 us -> 0 us
  Pallas kernels: 0 us -> 96.1 us
  between operations: 14 us -> 0.67 us
  starting transfers between devices: 7.12 us -> 0 us
    convert_element_type x10 -> x0, other arithmetic: 133 us -> none  [the longest x2 104 us: field_codes(): return (nibbles * spread).astype(jnp.bfloat16)]
    all_gather x4 -> x0, blocking collectives: 128 us -> none  [the longest x2 65 us: body(): gathered_rows = lax.all_gather(normed_part, 'head', axis=1, tiled=True)]
    reduce_scatter x2 -> x0, waiting for transfers between devices: 105 us -> none  [body(): lax.psum_scatter(partial_out, 'head', scatter_dimension=1, tiled=True)]
    dot_general x14 -> x0, matrix products: 105 us -> none  [the longest x2 30.3 us: body(): jnp.dot(hidden, down_weight, preferred_element_type=jnp.float32)]
    pallas_call x0 -> x1, Pallas kernels: none -> 96.1 us  [body(): pl.pallas_call(functools.partial(kernel, heads, blocks), out_shape=(jax.S...]
    shift_right_arithmetic x4 -> x0, local copies, waits for them, and re-layouts: 57.5 us -> none  [unpack_pairs(): jnp.right_shift(packed[:, None, :], shifts[None, :, None])]
    broadcast_in_dim x2, local copies, waits for them, and re-layouts: 52.4 us -> 0.75 us  [body(): lens = jnp.broadcast_to(lens, (inst, positions))]
    psum x1 -> x0, blocking collectives: 21.3 us -> none  [body(): squares = lax.psum(jnp.sum(stream_f * stream_f, axis=1), 'head')]
  transfers between devices with their start and end apart: 5 -> 0, of which waited for: 2 -> 0; matrix products, arithmetic and copies ran while one was open for 30% -> 0% of each run, Pallas kernels for 0% -> 0%
where the time goes in v1:
time: 104 us
  Pallas kernels  96.1 us (92%)
  local copies, waits for them, and re-layouts  5.49 us (5%)
  other arithmetic  1.27 us (1%)
    pallas_call x1, Pallas kernels, body(): pl.pallas_call(functools.partial(kernel, heads, blocks), out_shape=(jax.S...  96.1 us

profile of v1, /device:TPU:0, one launch (start us, length us, event | category | flops | bytes accessed | tf_op | source)
XLA Modules:
  0.0 103.6 jit_solution(9131396430746448454)
XLA Ops:
  0.6 0.0 copy-start
  0.7 0.6 copy-done
  1.3 0.1 constant_dynamic-slice_fusion
  1.4 0.1 broadcast_in_dim.7
  1.5 1.3 %reshape.44 = f32[1024]{0:T(1024)} convert(bf16[1024]{0:T(1024)(128)(2,1)} %param.15) | non-fusion elementwise | flops 1024 | bytes 6144 | tf_op jit(solution)/shard_map/reshape | solution.py:534
  2.7 0.7 broadcast_in_dim.8.len_ref
  3.4 1.3 %reshape.43.res_ref = f32[8,1024]{1,0:T(8,128)} reshape(bf16[2,4,1024]{2,1,0:T(4,128)(2,1)} %param.14) | data formatting | bytes 49152 | tf_op jit(solution)/shard_map/convert_element_type | solution.py:533
  4.7 96.1 %shard_map.149 = (bf16[8,1024]{1,0:T(8,128)(2,1)}, bf16[16,512]{1,0:T(8,128)(2,1)}) custom-call(f32[8,1024]{1,0:T(8,128)} %reshape.43.res_ref, f32[1,1024]{1,0:T(1,128)} %bitcast.13, bf16[8,8,128]{2,1,0:T(8,128)(2,1)} %bitcast.12, bf16[8,256,128]{2,1,0:T(8,128)(2,1)} %bitcast.9, bf16[8,256,128]{2,1,0:T(8,128)(2,1)} %bitcast.10, bf16[8,128]{1,0:T(8,128)(2,1)} %bitcast.14, ...), custom_call_target="tpu_custom_call" | custom-call | tf_op jit(solution)/shard_map/pallas_call | solution.py:541
  100.9 1.3 %reshape_transpose_reshape.4 = bf16[2,4,1024]{2,1,0:T(4,128)(2,1)} reshape(bf16[8,1024]{1,0:T(8,128)(2,1)} %get-tuple-element.4) | data formatting | bytes 32768 | tf_op jit(solution)/shard_map/reshape;transpose;reshape | solution.py:607
  102.2 0.7 reshape.41
  102.9 0.6 reshape.42
  (1 shorter events, 0.0 us)
Async XLA Ops:
  0.6 0.7 copy-start

commit v2 on v1

--- a/solution.py
+++ b/solution.py
@@ -15,6 +15,9 @@
 BF16 = jnp.bfloat16
 CHUNK = 256
 FTILE = 512
+DUNROLL = 16
+KUNROLL = 8
+PUNROLL = 8
 NT = (((1,), (1,)), ((), ()))
 
 
@@ -80,8 +83,8 @@
     inst = q_ref.shape[0]
     qper = q_ref.shape[1]
     positions = ck_ref.shape[1]
-    rows = res_ref.shape[0]
-    width = res_ref.shape[1]
+    rows = blocks * inst
+    width = res_ref.shape[2]
     both = 2 * rows
     feat = fp_ref.shape[0]
     hidden_units = fp_ref.shape[1]
@@ -238,18 +241,28 @@
             att_lhs[g * qper + k, block * inst : (block + 1) * inst, :] = part
 
     def project(gg, total):
-        for s in range(2):
-            g = gg * 2 + s
+        for s in range(PUNROLL):
+            g = gg * PUNROLL + s
             lhs = att_lhs[g]
             p = jnp.dot(lhs.astype(BF16), ocodes[g], preferred_element_type=F32)
             corr = 8.0 * jnp.sum(lhs, axis=1, keepdims=True)
             total = total + osf[pl.ds(g, 1), :] * (p - corr)
         return total
 
-    projected = lax.fori_loop(0, 2 * words // GROUP // 2, project, jnp.zeros((rows, width), F32))
-    stream = (res_ref[...] + projected).astype(BF16)
-    stream_ref[...] = stream
+    projected = lax.fori_loop(0, 2 * words // GROUP // PUNROLL, project, jnp.zeros((rows, width), F32))
+    micro = res_ref.shape[0]
+    slots = inst // micro
+    res = [res_ref[m].astype(F32) for m in range(micro)]
+    res = [
+        res[m][b * slots : (b + 1) * slots] for b in range(blocks) for m in range(micro)
+    ]
+    stream = (jnp.concatenate(res, axis=0) + projected).astype(BF16)
     stream_f = stream.astype(F32)
+    for m in range(micro):
+        firsts = [b * inst + m * slots for b in range(blocks)]
+        stream_ref[m] = jnp.concatenate(
+            [stream_f[first : first + slots] for first in firsts], axis=0
+        ).astype(BF16)
     sq_mine[...] = jnp.broadcast_to(
         jnp.sum(stream_f * stream_f, axis=1, keepdims=True), sq_mine.shape
     )
@@ -395,54 +408,66 @@
             for h in (h0, h1):
                 corr.append(8.0 * jnp.sum(h.astype(F32), axis=1, keepdims=True))
 
-        def dchunk(n, _):
-            first = pl.multiple_of(n * CHUNK, CHUNK)
-            total = acc_out[:, pl.ds(first, CHUNK)]
-            for pp in range(FTILE // 256):
-                codes = dcodes[slot, pl.ds(first, CHUNK), pp * 256 : (pp + 1) * 256]
-                p = lax.dot_general(lhs[pp], codes, NT, preferred_element_type=F32)
-                for s in range(2):
-                    g = j * (FTILE // GROUP) + pp * 2 + s
-                    row = dsf[pl.ds(g, 1), pl.ds(first, CHUNK)]
-                    total = total + row * (p[s * both : (s + 1) * both] - corr[pp * 2 + s])
-            acc_out[:, pl.ds(first, CHUNK)] = total
+        def dchunk(nn, _):
+            for u in range(DUNROLL):
+                first = pl.multiple_of((nn * DUNROLL + u) * CHUNK, CHUNK)
+                total = acc_out[:, pl.ds(first, CHUNK)]
+                for pp in range(FTILE // 256):
+                    codes = dcodes[slot, pl.ds(first, CHUNK), pp * 256 : (pp + 1) * 256]
+                    p = lax.dot_general(lhs[pp], codes, NT, preferred_element_type=F32)
+                    for s in range(2):
+                        g = j * (FTILE // GROUP) + pp * 2 + s
+                        row = dsf[pl.ds(g, 1), pl.ds(first, CHUNK)]
+                        total = total + row * (p[s * both : (s + 1) * both] - corr[pp * 2 + s])
+                acc_out[:, pl.ds(first, CHUNK)] = total
             return 0
 
-        lax.fori_loop(0, feat // CHUNK, dchunk, 0)
+        lax.fori_loop(0, feat // CHUNK // DUNROLL, dchunk, 0)
 
     def ftile(j, _):
         slot = lax.rem(j, 2)
         acc[slot] = jnp.zeros(acc.shape[1:], F32)
 
-        def chunk(k, _):
-            c = j * kchunks + k
-            rslot = lax.rem(c, ffn_slots)
-            ffn_copy(c).wait()
-            lhs = nbd[k]
-            n0 = jnp.concatenate([nsum[2 * k]] * 2, axis=1)
-            n1 = jnp.concatenate([nsum[2 * k + 1]] * 2, axis=1)
+        def chunk(kk, _):
+            ks = [kk * KUNROLL + u for u in range(KUNROLL)]
+            for k in ks:
+                ffn_copy(j * kchunks + k).wait()
             for n in range(FTILE // 256):
                 cols = slice(n * 256, (n + 1) * 256)
-                w = fring[rslot, :, cols]
                 at = pl.ds(pl.multiple_of(j * FTILE + n * 256, 256), 256)
-                dcodes[slot, pl.ds(pl.multiple_of(k * CHUNK, CHUNK), CHUNK), cols] = (
-                    (w >> 8).astype(F32).astype(BF16)
-                )
-                for which, scales in ((0, gsf), (1, usf)):
-                    bits = (w & 15) if which == 0 else ((w >> 4) & 15)
-                    p = jnp.dot(lhs, bits.astype(F32).astype(BF16), preferred_element_type=F32)
-                    acc[slot, which, :, cols] += (
-                        scales[pl.ds(2 * k, 1), at] * (p[:both] - n0)
-                        + scales[pl.ds(2 * k + 1, 1), at] * (p[both:] - n1)
+                totals = [acc[slot, 0, :, cols], acc[slot, 1, :, cols]]
+                for k in ks:
+                    rslot = lax.rem(j * kchunks + k, ffn_slots)
+                    lhs = nbd[k]
+                    n0 = jnp.concatenate([nsum[2 * k]] * 2, axis=1)
+                    n1 = jnp.concatenate([nsum[2 * k + 1]] * 2, axis=1)
+                    w = fring[rslot, :, cols]
+                    dcodes[slot, pl.ds(pl.multiple_of(k * CHUNK, CHUNK), CHUNK), cols] = (
+                        (w >> 8).astype(F32).astype(BF16)
                     )
-
-            @pl.when(c + ffn_slots < total_chunks)
-            def _():
-                ffn_copy(c + ffn_slots).start()
+                    sums = [
+                        jnp.dot(lhs, (w & most).astype(F32).astype(BF16), preferred_element_type=F32)
+                        for most in (15, 255)
+                    ]
+                    sums[1] = (sums[1] - sums[0]) * 0.0625
+                    for which, scales in ((0, gsf), (1, usf)):
+                        p = sums[which]
+                        totals[which] = totals[which] + (
+                            scales[pl.ds(2 * k, 1), at] * (p[:both] - n0)
+                            + scales[pl.ds(2 * k + 1, 1), at] * (p[both:] - n1)
+                        )
+                acc[slot, 0, :, cols] = totals[0]
+                acc[slot, 1, :, cols] = totals[1]
+            for k in ks:
+                c = j * kchunks + k
+
+                @pl.when(c + ffn_slots < total_chunks)
+                def _():
+                    ffn_copy(c + ffn_slots).start()
 
             return 0
 
-        lax.fori_loop(0, kchunks, chunk, 0)
+        lax.fori_loop(0, kchunks // KUNROLL, chunk, 0)
         part_send[j] = acc[slot].astype(BF16)
         part_copy(j).start()
 
@@ -455,7 +480,7 @@
     lax.fori_loop(0, ftiles, ftile, 0)
     down(ftiles - 1)
 
-    share = out_ref.shape[1]
+    share = out_ref.shape[2]
     for t in range(heads):
         rs_send[t] = acc_out[:, t * share : (t + 1) * share].astype(BF16)
 
@@ -494,7 +519,11 @@
     result = rs_recv[0].astype(F32)
     for t in range(1, heads):
         result = result + rs_recv[t].astype(F32)
-    out_ref[...] = result.astype(BF16)
+    for m in range(micro):
+        firsts = [b * inst + m * slots for b in range(2 * blocks)]
+        out_ref[m] = jnp.concatenate(
+            [result[first : first + slots] for first in firsts], axis=0
+        ).astype(BF16)
 
 
 def body(
@@ -529,8 +558,6 @@
     first_row = unit // KV_HEADS * slots
     lens = lax.dynamic_slice_in_dim(lengths, first_row, slots, axis=1).reshape(inst, 1)
     lens = jnp.broadcast_to(lens, (inst, positions))
-    res = residual.reshape(micro, blocks, slots, width).transpose(1, 0, 2, 3)
-    res = res.reshape(rows, width).astype(F32)
     gain = norm_gain.astype(F32).reshape(1, width)
     out_slots = min(8, words // CHUNK)
     ffn_slots = min(16, (feat // CHUNK) * ftiles)
@@ -541,8 +568,8 @@
     stream, out = pl.pallas_call(
         functools.partial(kernel, heads, blocks),
         out_shape=(
-            jax.ShapeDtypeStruct((rows, width), BF16),
-            jax.ShapeDtypeStruct((both, share), BF16),
+            jax.ShapeDtypeStruct(residual.shape, BF16),
+            jax.ShapeDtypeStruct((micro, 2 * blocks * slots, share), BF16),
         ),
         in_specs=[vmem] * 8 + [anywhere, vmem, anywhere, vmem, vmem, vmem],
         out_specs=(vmem, vmem),
@@ -588,7 +615,7 @@
             collective_id=0, has_side_effects=True, vmem_limit_bytes=58 * 1024 * 1024
         ),
     )(
-        res,
+        residual,
         gain,
         queries.reshape(inst, qper, hd),
         cache_keys.reshape(inst, positions, hd),
@@ -603,10 +630,6 @@
         up_scales,
         down_scales,
     )
-    stream = stream.reshape(blocks, micro, slots, width).transpose(1, 0, 2, 3)
-    stream = stream.reshape(micro, blocks * slots, width)
-    out = out.reshape(2, blocks, micro, slots, share).transpose(2, 0, 1, 3, 4)
-    out = out.reshape(micro, 2 * blocks * slots, share)
     return (stream, out)
 
 

time: 104 us -> 72.7 us (0.70)
  Pallas kernels: 96.1 us -> 66.3 us
  local copies, waits for them, and re-layouts: 5.49 us -> 4.13 us
    pallas_call x1, Pallas kernels: 96.1 us -> 66.3 us  [body(): pl.pallas_call(functools.partial(kernel, heads, blocks), out_shape=(jax.S...]
    unnamed x2 -> x4, local copies, waits for them, and re-layouts: 0.66 us -> 3.31 us
    reshape x2 -> x0, local copies, waits for them, and re-layouts: 1.35 us -> none  [the longest x1 0.73 us: body(): out = out.reshape(2, blocks, micro, slots, share).transpose(2, 0, 1, 3, 4)]
    another operation x1 -> x0, local copies, waits for them, and re-layouts: 1.34 us -> none  [body(): stream = stream.reshape(micro, blocks * slots, width)]
    convert_element_type x1 -> x0, local copies, waits for them, and re-layouts: 1.32 us -> none  [body(): res = res.reshape(rows, width).astype(F32)]
where the time goes in v2:
time: 72.7 us; the launch traced here: 72.3 us
  Pallas kernels  66.3 us (91%)
  local copies, waits for them, and re-layouts  4.13 us (6%)
  other arithmetic  1.27 us (2%)
    pallas_call x1, Pallas kernels, body(): pl.pallas_call(functools.partial(kernel, heads, blocks), out_shape=(jax.S...  66.3 us
    unnamed x4, local copies, waits for them, and re-layouts  3.31 us

profile of v2, /device:TPU:0, one launch (start us, length us, event | category | flops | bytes accessed | tf_op | source)
XLA Modules:
  0.0 72.3 jit_solution(10109835755919236341)
XLA Ops:
  0.6 0.0 copy-start
  0.7 0.6 copy-done
  1.3 0.1 constant_dynamic-slice_fusion
  1.4 0.1 broadcast_in_dim.7
  1.5 1.3 %reshape.33 = f32[1024]{0:T(1024)} convert(bf16[1024]{0:T(1024)(128)(2,1)} %param.15) | non-fusion elementwise | flops 1024 | bytes 6144 | tf_op jit(solution)/shard_map/reshape | solution.py:561
  2.7 0.7 broadcast_in_dim.8.len_ref
  3.4 66.3 %shard_map.149 = (bf16[2,4,1024]{2,1,0:T(4,128)(2,1)}, bf16[2,8,512]{2,1,0:T(8,128)(2,1)}) custom-call(bf16[2,4,1024]{2,1,0:T(4,128)(2,1)} %res_ref.1, f32[1,1024]{1,0:T(1,128)} %bitcast.8, bf16[8,8,128]{2,1,0:T(8,128)(2,1)} %bitcast.9, bf16[8,256,128]{2,1,0:T(8,128)(2,1)} %bitcast.6, bf16[8,256,128]{2,1,0:T(8,128)(2,1)} %bitcast.7, ...), custom_call_target="tpu_custom_call" | custom-call | tf_op jit(solution)/shard_map/pallas_call | solution.py:568
  69.7 1.3 %copy.18 = bf16[2,4,1024]{2,1,0:T(4,128)(2,1)} copy(bf16[2,4,1024]{2,1,0:T(4,128)(2,1)} %get-tuple-element.4) | data formatting | bytes 32768
  71.0 1.3 %copy.19 = bf16[2,8,512]{2,1,0:T(8,128)(2,1)} copy(bf16[2,8,512]{2,1,0:T(8,128)(2,1)} %get-tuple-element.5) | data formatting | bytes 32768
Async XLA Ops:
  0.6 0.7 copy-start
